TPU v7x, 32 devices: a whole 2x2x4 slice. The times are simulated.
32 devices in a mesh: group: 2 (over y), hid: 16 (over z, x, core).
Axes of the slice: x: 2, y: 2, z: 4, core: 2. Of those that a mesh axis runs over, the one named last changes fastest.
Arguments:
- tokens: bfloat16 [64, 8192], P(('group', 'hid')), parts along dimension 0, may hold values from -48 to 48
- norm_gain: bfloat16 [8192], replicated, may hold values from 0.099609375 to 1.8984375
- curve_point: float32 [1], replicated, may hold values from 0.25 to 0.75
- gate_tiles: bfloat16 [3, 16, 36, 128, 128], P(None, 'hid'), may hold values from -0.1875 to 0.1875
- up_tiles: bfloat16 [3, 16, 36, 128, 128], P(None, 'hid'), may hold values from -0.1875 to 0.1875
- down_tiles: bfloat16 [3, 16, 36, 128, 128], P(None, 'hid'), may hold values from -0.375 to 0.375
- gate_index: int32 [3, 16, 36], P(None, 'hid'), may hold values from 0 to 63, as said below
- up_index: int32 [3, 16, 36], P(None, 'hid'), may hold values from 0 to 63, as said below
- down_index: int32 [3, 16, 36], P(None, 'hid'), may hold values from 0 to 63, as said below
- kept_counts: int32 [3, 3, 16], P(None, None, 'hid'), may hold values from 16 to 36, as said below
Outputs:
- ffn_out: bfloat16 [64, 8192], P(('group', 'hid')), parts along dimension 0
There are 2 independent parts, one for each index of `group`. A program takes and returns all parts, laid end to end along the dimension named above; an argument that names none is the same for every part. Nothing has to cross between parts.
Inputs may be any that keep to these rules, and one draw needn't show every extreme that they name: `kept_counts`: for each matrix and control point, some hidden block column holds exactly 36 kept blocks; which column that is may differ from one matrix and control point to another. `gate_index`: the entries of one list are distinct; only the first kept_counts entries of a list name kept blocks, the others are ignored. `up_index`: as gate_index. `down_index`: as gate_index.
All inputs are finite; a program needn't handle non-finite values.
Results may differ from a plain program's by a relative error of at most 0.0064.
Values may be sent and summed in bfloat16 or wider, within the bound.
A program may use at most 128 MiB of HBM per device.

v0:
```python
import jax
import jax.numpy as jnp
from jax import lax
from jax.sharding import PartitionSpec as P

EPS = 1e-05


def packed_in(blocks, tile_set, block_ids, keep_mask):
    chosen = jnp.take(blocks, block_ids, axis=1)
    chosen = jnp.where(keep_mask[None, :, None], chosen, jnp.zeros((), chosen.dtype))
    return jnp.einsum("rsk,skh->rh", chosen, tile_set, preferred_element_type=jnp.float32)


def packed_out(hidden_part, tile_set, block_ids, keep_mask, factor, running):
    product = jnp.einsum("rh,sho->rso", hidden_part, tile_set, preferred_element_type=jnp.float32)
    product = jnp.where(keep_mask[None, :, None], factor * product, 0.0)
    return running.at[:, block_ids].add(product)


def shards(
    tokens,
    norm_gain,
    curve_point,
    gate_tiles,
    up_tiles,
    down_tiles,
    gate_index,
    up_index,
    down_index,
    kept_counts,
):
    feature_width = tokens.shape[1]
    block_size = gate_tiles.shape[-1]
    column_blocks = feature_width // block_size
    capacity = gate_tiles.shape[2]
    tokens_f32 = tokens.astype(jnp.float32)
    mean_square = jnp.mean(tokens_f32 * tokens_f32, axis=-1, keepdims=True)
    normed = (tokens_f32 * lax.rsqrt(mean_square + EPS) * norm_gain.astype(jnp.float32)).astype(
        jnp.bfloat16
    )
    point = curve_point[0]
    blend_coef = ((1.0 - point) * (1.0 - point), 2.0 * point * (1.0 - point), point * point)
    slot_ids = jnp.arange(capacity, dtype=jnp.int32)
    keep_masks = [
        [slot_ids < kept_counts[matrix_id, control, 0] for control in range(3)]
        for matrix_id in range(3)
    ]
    piece_rows = lax.all_gather(normed, "hid", axis=0, tiled=True)
    blocks = piece_rows.reshape(piece_rows.shape[0], column_blocks, block_size)
    gate_sum = jnp.zeros((piece_rows.shape[0], block_size), jnp.float32)
    up_sum = jnp.zeros((piece_rows.shape[0], block_size), jnp.float32)
    for control in range(3):
        gate_sum = gate_sum + blend_coef[control] * packed_in(
            blocks, gate_tiles[control, 0], gate_index[control, 0], keep_masks[0][control]
        )
        up_sum = up_sum + blend_coef[control] * packed_in(
            blocks, up_tiles[control, 0], up_index[control, 0], keep_masks[1][control]
        )
    hidden = (jax.nn.silu(gate_sum) * up_sum).astype(jnp.bfloat16)
    running = jnp.zeros((hidden.shape[0], column_blocks, block_size), jnp.float32)
    for control in range(3):
        running = packed_out(
            hidden,
            down_tiles[control, 0],
            down_index[control, 0],
            keep_masks[2][control],
            blend_coef[control],
            running,
        )
    summed = lax.psum_scatter(
        running.reshape(hidden.shape[0], feature_width), "hid", scatter_dimension=0, tiled=True
    )
    return summed.astype(jnp.bfloat16)


def solution(mesh):
    return jax.shard_map(
        shards,
        mesh=mesh,
        in_specs=(
            P(("group", "hid"), None),
            P(),
            P(),
            P(None, "hid", None, None, None),
            P(None, "hid", None, None, None),
            P(None, "hid", None, None, None),
            P(None, "hid", None),
            P(None, "hid", None),
            P(None, "hid", None),
            P(None, None, "hid"),
        ),
        out_specs=P(("group", "hid"), None),
        check_vma=False,
    )
```

profile of v0, /device:TPU:0, one launch (start us, length us, event | category | flops | bytes accessed | tf_op | source)
XLA Modules:
  0.0 134.1 jit_solution(13446687820629276260)
XLA Ops:
  0.0 0.7 convert_element_type.16
  0.7 0.9 fusion.117
  1.7 0.9 fusion.120
  2.5 24.6 %all-gather = bf16[16,2,8192]{2,1,0:T(2,128)(2,1)S(1)} all-gather(bf16[1,2,8192]{2,1,0:T(2,128)(2,1)S(1)} %fusion.120), channel_id=1, replica_groups=mesh['group'=2,'hid'=16] {'hid'}, dimensions={0}, use_global_device_ids=true | all-gather | bytes 557056 | tf_op jit(solution)/shard_map/all_gather | solution.py:49
  27.9 0.7 compare_and_fusion.3
  28.6 0.6 gather_fusion
  29.2 1.5 %fusion.136 = (s32[1,1,1]{1,2,0:T(1,128)}, s32[1,1,1]{1,2,0:T(1,128)}, s32[1,1,1]{1,2,0:T(1,128)}, s32[1,1,1]{1,2,0:T(1,128)}, s32[1,1,1]{1,2,0:T(1,128)}, /*ind...) fusion(s32[3,3,1]{1,2,0:T(1,128)} %param.21), kind=kLoop, calls=%fused_computation.151 | loop fusion | bytes 72 | tf_op jit(solution)/shard_map/slice | solution.py:46
  30.7 0.7 iota_compare_fusion.7
  32.1 1.6 %fusion.78 = f32[32,128]{1,0:T(8,128)S(1)} fusion(bf16[3,1,36,128,128]{4,3,2,1,0:T(8,128)(2,1)} %param.15, bf16[36,32,128]{2,1,0:T(8,128)(2,1)S(1)} %gather_fusion, pred[36]{0:T(512)(128)(4,1)S(1)} %get-tuple-element.30, pred[36]{0:T(512)(128)(4,1)S(1)} %iota_compare_fusion.7, f32[]{:T(128)} %bitcast.3), kind=kOutput, calls=%fused_computation.58 | convolution fusion | flops 38047744 | bytes 1491528 | tf_op jit(solution)/shard_map/rsk,skh->rh/dot_general | solution.py:12
  33.7 0.6 gather_fusion.1
  34.9 1.6 %fusion.75 = f32[32,128]{1,0:T(8,128)S(1)} fusion(f32[32,128]{1,0:T(8,128)S(1)} %fusion.78, bf16[3,1,36,128,128]{4,3,2,1,0:T(8,128)(2,1)} %param.15, bf16[36,32,128]{2,1,0:T(8,128)(2,1)S(1)} %gather_fusion.1, pred[36]{0:T(512)(128)(4,1)S(1)} %get-tuple-element.32, pred[36]{0:T(512)(128)(4,1)S(1)} %iota_compare_fusion.6, f32[]{:T(128)} %bitcast.10), kind=kOutput, calls=%fused_computation.57 | convolution fusion | flops 38051840 | bytes 1507912 | tf_op jit(solution)/shard_map/rsk,skh->rh/dot_general | solution.py:12
  36.5 0.6 gather_fusion.2
  37.1 0.6 iota_compare_fusion.5
  37.8 1.6 %fusion.69 = f32[32,128]{1,0:T(8,128)S(1)} fusion(f32[32,128]{1,0:T(8,128)S(1)} %fusion.75, bf16[3,1,36,128,128]{4,3,2,1,0:T(8,128)(2,1)} %param.15, bf16[36,32,128]{2,1,0:T(8,128)(2,1)S(1)} %gather_fusion.2, pred[36]{0:T(512)(128)(4,1)S(1)} %get-tuple-element.6, pred[36]{0:T(512)(128)(4,1)S(1)} %iota_compare_fusion.5, f32[]{:T(128)} %bitcast.16), kind=kOutput, calls=%fused_computation.55 | convolution fusion | flops 38051840 | bytes 1507912 | tf_op jit(solution)/shard_map/rsk,skh->rh/dot_general | solution.py:12
  39.4 0.6 gather_fusion.3
  40.0 0.6 iota_compare_fusion.4
  40.7 1.6 %fusion.63 = f32[32,128]{1,0:T(8,128)S(1)} fusion(bf16[3,1,36,128,128]{4,3,2,1,0:T(8,128)(2,1)} %param.16, bf16[36,32,128]{2,1,0:T(8,128)(2,1)S(1)} %gather_fusion.3, pred[36]{0:T(512)(128)(4,1)S(1)} %get-tuple-element.34, pred[36]{0:T(512)(128)(4,1)S(1)} %iota_compare_fusion.4, f32[]{:T(128)} %bitcast.3), kind=kOutput, calls=%fused_computation.53 | convolution fusion | flops 38047744 | bytes 1491528 | tf_op jit(solution)/shard_map/rsk,skh->rh/dot_general | solution.py:12
  42.3 0.6 gather_fusion.4
  43.0 0.6 iota_compare_fusion.3
  43.6 1.6 %fusion.60 = f32[32,128]{1,0:T(8,128)S(1)} fusion(f32[32,128]{1,0:T(8,128)S(1)} %fusion.63, bf16[3,1,36,128,128]{4,3,2,1,0:T(8,128)(2,1)} %param.16, bf16[36,32,128]{2,1,0:T(8,128)(2,1)S(1)} %gather_fusion.4, pred[36]{0:T(512)(128)(4,1)S(1)} %get-tuple-element.36, pred[36]{0:T(512)(128)(4,1)S(1)} %iota_compare_fusion.3, f32[]{:T(128)} %bitcast.10), kind=kOutput, calls=%fused_computation.52 | convolution fusion | flops 38051840 | bytes 1507912 | tf_op jit(solution)/shard_map/rsk,skh->rh/dot_general | solution.py:12
  46.4 1.6 %fusion.84 = bf16[32,128,1]{1,0,2:T(8,128)(2,1)S(1)} fusion(f32[32,128]{1,0:T(8,128)S(1)} %fusion.60, bf16[3,1,36,128,128]{4,3,2,1,0:T(8,128)(2,1)} %param.16, bf16[36,32,128]{2,1,0:T(8,128)(2,1)S(1)} %gather_fusion.5, pred[36]{0:T(512)(128)(4,1)S(1)} %get-tuple-element.12, pred[36]{0:T(512)(128)(4,1)S(1)} %iota_compare_fusion.2, ...), kind=kOutput, calls=%fused_computation.60 | convolution fusion | flops 38076416 | bytes 1516104 | tf_op jit(solution)/shard_map/rsk,skh->rh/dot_general | solution.py:12
  48.1 0.6 iota_compare_fusion.8
  48.7 1.6 %fusion.1 = f32[36,32,128]{2,1,0:T(8,128)S(1)} fusion(bf16[32,128,1]{1,0,2:T(8,128)(2,1)S(1)} %fusion.84, bf16[3,1,36,128,128]{4,3,2,1,0:T(8,128)(2,1)} %param.17, f32[]{:T(128)} %bitcast.3, pred[36]{0:T(512)(128)(4,1)S(1)} %iota_compare_fusion.8), kind=kOutput, calls=%fused_computation.13 | convolution fusion | flops 38043648 | bytes 1778212 | tf_op jit(solution)/shard_map/rh,sho->rso/dot_general | solution.py:16
  50.4 2.6 %scatter_fusion = f32[32,64,128]{2,0,1:T(8,128)S(1)} fusion(f32[32,64,128]{2,0,1:T(8,128)S(1)} %broadcast_in_dim.92, s32[36]{0:T(128)S(1)} %get-tuple-element.28, f32[36,32,128]{2,1,0:T(8,128)S(1)} %fusion.1), kind=kCustom, calls=%fused_computation.6 | custom fusion | flops 147456 | bytes 1769616 | tf_op jit(solution)/shard_map/scatter-add | solution.py:18
  53.0 0.7 iota_compare_fusion.1
  53.7 1.6 %fusion.3 = f32[36,32,128]{2,1,0:T(8,128)S(1)} fusion(bf16[32,128,1]{1,0,2:T(8,128)(2,1)S(1)} %fusion.84, bf16[3,1,36,128,128]{4,3,2,1,0:T(8,128)(2,1)} %param.17, f32[]{:T(128)} %bitcast.10, pred[36]{0:T(512)(128)(4,1)S(1)} %iota_compare_fusion.1), kind=kOutput, calls=%fused_computation.15 | convolution fusion | flops 38043648 | bytes 1778212 | tf_op jit(solution)/shard_map/rh,sho->rso/dot_general | solution.py:16
  55.2 2.6 %scatter_fusion.1 = f32[32,64,128]{2,0,1:T(8,128)S(1)} fusion(f32[32,64,128]{2,0,1:T(8,128)S(1)} %scatter_fusion, s32[36]{0:T(128)S(1)} %get-tuple-element.29, f32[36,32,128]{2,1,0:T(8,128)S(1)} %fusion.3), kind=kCustom, calls=%fused_computation.7 | custom fusion | flops 147456 | bytes 1769616 | tf_op jit(solution)/shard_map/scatter-add | solution.py:18
  57.8 0.7 iota_compare_fusion
  58.5 1.6 %fusion.5 = f32[36,32,128]{2,1,0:T(8,128)S(1)} fusion(bf16[32,128,1]{1,0,2:T(8,128)(2,1)S(1)} %fusion.84, bf16[3,1,36,128,128]{4,3,2,1,0:T(8,128)(2,1)} %param.17, f32[]{:T(128)} %bitcast.16, pred[36]{0:T(512)(128)(4,1)S(1)} %iota_compare_fusion), kind=kOutput, calls=%fused_computation.17 | convolution fusion | flops 38043648 | bytes 1778212 | tf_op jit(solution)/shard_map/rh,sho->rso/dot_general | solution.py:16
  60.0 2.6 %scatter_fusion.2 = f32[32,64,128]{2,0,1:T(8,128)S(1)} fusion(f32[32,64,128]{2,0,1:T(8,128)S(1)} %scatter_fusion.1, s32[36]{0:T(128)S(1)} %get-tuple-element.27, f32[36,32,128]{2,1,0:T(8,128)S(1)} %fusion.5), kind=kCustom, calls=%fused_computation.8 | custom fusion | flops 147456 | bytes 1769616 | tf_op jit(solution)/shard_map/scatter-add | solution.py:18
  62.7 69.5 %all-reduce.2 = bf16[32,8192]{1,0:T(8,128)(2,1)S(1)} all-reduce(f32[32,8192]{1,0:T(8,128)S(1)} %copy_bitcast_fusion), channel_id=2, replica_groups=mesh['group'=2,'hid'=16] {'hid'}, use_global_device_ids=true, to_apply=%region_4.6.clone | all-reduce | flops 262144 | bytes 1572864
  133.5 0.7 dynamic-slice_convert_fusion
  (21 shorter events, 3.3 us)
Async XLA Ops:
  32.0 7.4 %copy-start.1 = (s32[3,1,36]{2,1,0:T(1,128)S(1)}, s32[3,1,36]{2,1,0:T(1,128)}, u32[]{:S(2)}) copy-start(s32[3,1,36]{2,1,0:T(1,128)} %param.19) | copy-start | bytes 1300
  42.3 7.9 %copy-start = (s32[3,1,36]{2,1,0:T(1,128)S(1)}, s32[3,1,36]{2,1,0:T(1,128)}, u32[]{:S(2)}) copy-start(s32[3,1,36]{2,1,0:T(1,128)} %param.20) | copy-start | bytes 1300
  58.5 73.8 %copy-start.2 = (u32[32]{0:T(128)S(1)}, u32[32]{0:T(128)}, u32[]{:S(2)}) copy-start(u32[32]{0:T(128)} %constant.43) | copy-start | bytes 388
where the time goes:
time: 135 us; the launch traced here: 134 us
  blocking collectives  94.1 us (70%)
  other arithmetic  16.7 us (12%)
  matrix products  14.4 us (11%)
  local copies, waits for them, and re-layouts  7.3 us (5%)
  between operations  1.63 us (1%)
    unnamed x1, blocking collectives  69.5 us
    all_gather x1, blocking collectives, shards(): piece_rows = lax.all_gather(normed, 'hid', axis=0, tiled=True)  24.6 us
    dot_general x6, matrix products, packed_in(): jnp.einsum('rsk,skh->rh', chosen, tile_set, preferred_element_type=jnp.fl...  9.74 us
    scatter-add x3, other arithmetic, packed_out(): return running.at[:, block_ids].add(product)  7.71 us
    lt x9, other arithmetic, shards(): slot_ids < kept_counts[matrix_id, control, 0]  5.67 us
    dot_general x3, matrix products, packed_out(): jnp.einsum('rh,sho->rso', hidden_part, tile_set, preferred_element_type=j...  4.69 us
    gather x6, local copies, waits for them, and re-layouts, packed_in(): chosen = jnp.take(blocks, block_ids, axis=1)  3.62 us

commit v1 on v0

v1 whole, which is shorter than its diff:
```python
import functools

import jax
import jax.numpy as jnp
from jax import lax
from jax.experimental import pallas as pl
from jax.experimental.pallas import tpu as pltpu
from jax.sharding import PartitionSpec as P

EPS = 1e-05
MESH = pl.DeviceIdType.MESH
F32 = jnp.float32
BF16 = jnp.bfloat16


def each(count, body):
    if count <= 8:
        for i in range(count):
            body(i)
    else:

        def step(i, carry):
            body(i)
            return carry

        lax.fori_loop(0, count, step, 0)


def kernel(
    n,
    chunks,
    tok,
    gain,
    point_ref,
    gate_idx,
    up_idx,
    down_idx,
    counts,
    gate_hbm,
    up_hbm,
    down_hbm,
    out,
    gate_w,
    up_w,
    down_w,
    gathered,
    stage,
    blocks,
    final,
    s1,
    r1,
    s2,
    r2,
    s3,
    r3,
    inv_v,
    inv_s,
    w_sem,
    inv_sem,
    ga_s,
    ga_r,
    gb_s,
    gb_r,
    gc_s,
    gc_r,
    s1_s,
    s1_r,
    s2_s,
    s2_r,
    s3_s,
    s3_r,
):
    rows, width = tok.shape
    blk = gate_w.shape[-1]
    nb = width // blk
    cap = gate_w.shape[1]
    msg = nb * rows
    part = msg // chunks
    na = n // 4
    half = n // 2

    h = lax.axis_index("hid")
    core = lax.rem(h, 2)
    b = lax.rem(h // 2, 2)
    a = h // 4

    def place(core_, b_, a_):
        return (core_ * 2 + b_) * na + a_

    def peer(a_, b_, core_):
        return {"hid": a_ * 4 + b_ * 2 + core_}

    core_peer = peer(a, b, 1 - core)
    b_peer = peer(a, 1 - b, core)
    me = place(core, b, a)

    def remote(src, dst, send, recv, to):
        return pltpu.make_async_remote_copy(
            src_ref=src, dst_ref=dst, send_sem=send, recv_sem=recv, device_id=to, device_id_type=MESH
        )

    loads = []
    for m, (src, dst) in enumerate(((gate_hbm, gate_w), (up_hbm, up_w))):
        for c in range(3):
            loads.append(pltpu.make_async_copy(src.at[c, 0], dst.at[c], w_sem.at[m, c]))
    for c in range(3):
        loads.append(
            pltpu.make_async_copy(down_hbm.at[c, 0], down_w.at[pl.ds(c * cap, cap)], w_sem.at[2, c])
        )
    for copy in loads:
        copy.start()

    barrier = pltpu.get_barrier_semaphore()

    def greet(i):
        to = peer(lax.rem(a + 1 + i, na), b, core)
        pl.semaphore_signal(barrier, inc=1, device_id=to, device_id_type=MESH)

    each(na - 1, greet)
    pl.semaphore_signal(barrier, inc=1, device_id=b_peer, device_id_type=MESH)
    pl.semaphore_signal(barrier, inc=1, device_id=core_peer, device_id_type=MESH)

    x = tok[...].astype(F32)
    mean_square = jnp.sum(x * x, axis=-1, keepdims=True) / width
    x = x * lax.rsqrt(mean_square + EPS) * gain[...].astype(F32)
    for r in range(nb):
        final[r * rows : (r + 1) * rows, :] = x[:, r * blk : (r + 1) * blk]
    gathered[me] = final[...].astype(BF16)

    pl.semaphore_wait(barrier, na + 1)

    def copy_a(i):
        blk_ref = gathered.at[me]
        return remote(blk_ref, blk_ref, ga_s.at[i], ga_r.at[i], peer(lax.rem(a + 1 + i, na), b, core))

    def copy_b(i):
        blk_ref = gathered.at[place(core, b, lax.rem(a - i + na, na))]
        return remote(blk_ref, blk_ref, gb_s.at[i], gb_r.at[i], b_peer)

    def copy_c(i, b_):
        at = place(core, b if b_ == 0 else 1 - b, lax.rem(a - i + na, na))
        blk_ref = gathered.at[at]
        sem = i + b_ * na
        return remote(blk_ref, blk_ref, gc_s.at[sem], gc_r.at[sem], core_peer)

    def got_a(i):
        ref = gathered.at[place(core, b, lax.rem(a - 1 - i + na, na))]
        remote(ref, ref, ga_s.at[i], ga_r.at[i], b_peer).wait_recv()

    def got_b(i):
        ref = gathered.at[place(core, 1 - b, lax.rem(a - i + na, na))]
        remote(ref, ref, gb_s.at[i], gb_r.at[i], b_peer).wait_recv()

    def got_c(i, b_):
        ref = gathered.at[place(1 - core, b if b_ == 0 else 1 - b, lax.rem(a - i + na, na))]
        sem = i + b_ * na
        remote(ref, ref, gc_s.at[sem], gc_r.at[sem], core_peer).wait_recv()

    copy_b(0).start()
    each(na - 1, lambda i: copy_a(i).start())
    copy_c(0, 0).start()

    zero_tile = 3 * cap
    lane = lax.broadcasted_iota(jnp.int32, (8, 128), 1)
    line = lax.broadcasted_iota(jnp.int32, (8, 128), 0)
    table = jnp.full((8, 128), zero_tile, jnp.int32)
    for c in range(3):
        kept = counts[2, c, 0]
        row = jnp.full((8, 128), zero_tile, jnp.int32)
        for s in range(cap):
            target = jnp.where(s < kept, down_idx[c, 0, s], -1)
            row = jnp.where(lane == target, c * cap + s, row)
        table = jnp.where(line == c, row, table)
    inv_v[...] = table
    inv_copy = pltpu.make_async_copy(inv_v, inv_s, inv_sem)
    inv_copy.start()
    blocks[nb] = jnp.zeros(blocks.shape[1:], BF16)
    down_w[zero_tile] = jnp.zeros((blk, blk), BF16)

    def on_a(i):
        got_a(i)
        copy_b(i + 1).start()
        copy_c(i + 1, 0).start()

    each(na - 1, on_a)

    def on_b(i):
        got_b(i)
        copy_c(i, 1).start()

    each(na, on_b)
    each(na, lambda i: got_c(i, 0))
    each(na, lambda i: got_c(i, 1))

    def widen(p):
        stage[pl.ds(p * msg, msg), :] = gathered[p].astype(F32)

    each(n, widen)

    def regroup(g):
        for d in range(8):
            r = g * 8 + d
            for t in range(rows):
                blocks[r, t * n : (t + 1) * n, :] = stage[pl.ds(r * rows + t, n, stride=msg), :].astype(BF16)

    each(nb // 8, regroup)

    point = point_ref[0]
    coef = ((1.0 - point) * (1.0 - point), 2.0 * point * (1.0 - point), point * point)

    def project(m, idx, w):
        total = jnp.zeros((rows * n, blk), F32)
        group = 12
        for c in range(3):
            loads[m * 3 + c].wait()
            kept = counts[m, c, 0]
            acc = jnp.zeros((rows * n, blk), F32)
            for g in range(0, cap, group):
                size = min(group, cap - g)
                left = jnp.concatenate(
                    [blocks[jnp.where(s < kept, idx[c, 0, s], nb)] for s in range(g, g + size)], axis=1
                )
                right = w[c, g : g + size].reshape(size * blk, blk)
                acc = acc + jnp.dot(left, right, preferred_element_type=F32)
            total = total + coef[c] * acc
        return total

    gate = project(0, gate_idx, gate_w)
    up = project(1, up_idx, up_w)
    hidden = (gate / (1.0 + jnp.exp(-gate)) * up).astype(BF16)

    for copy in loads[6:]:
        copy.wait()
    inv_copy.wait()

    per = nb // chunks

    def down(k):
        def some(g):
            for d in range(4):
                r = k * per + g * 4 + d
                total = jnp.zeros((rows * n, blk), F32)
                for c in range(3):
                    total = total + coef[c] * jnp.dot(hidden, down_w[inv_s[c, r]], preferred_element_type=F32)
                for t in range(rows):
                    stage[pl.ds(r * rows + t, n, stride=msg), :] = total[t * n : (t + 1) * n]

        each(per // 4, some)

    def piece(p, k):
        return stage[pl.ds(pl.multiple_of(p * msg + k * part, part), part), :]

    def send1(k):
        return remote(s1.at[k], r1.at[k], s1_s.at[k], s1_r.at[k], core_peer)

    def send2(k):
        return remote(s2.at[k], r2.at[k], s2_s.at[k], s2_r.at[k], b_peer)

    def send3(k, i):
        to = peer(lax.rem(a + 1 + i, na), b, core)
        return remote(s3.at[k, i], r3.at[k, i], s3_s.at[k, i], s3_r.at[k, i], to)

    def step1(k):
        down(k)

        def pack(q):
            s1[k, q] = piece((1 - core) * half + q, k).astype(BF16)

        each(half, pack)
        send1(k).start()

    def step2(k):
        send1(k).wait_recv()

        def pack(q):
            at = (1 - b) * na + q
            s2[k, q] = (piece(core * half + at, k) + r1[k, at].astype(F32)).astype(BF16)

        each(na, pack)
        send2(k).start()

    def step3(k):
        send2(k).wait_recv()

        def value(q):
            at = b * na + q
            return piece(core * half + at, k) + r1[k, at].astype(F32) + r2[k, q].astype(F32)

        def pack(i):
            s3[k, i] = value(lax.rem(a + 1 + i, na)).astype(BF16)
            send3(k, i).start()

        each(na - 1, pack)
        final[k * part : (k + 1) * part, :] = value(a)

    def step4(k):
        def add(i):
            send3(k, i).wait_recv()
            final[k * part : (k + 1) * part, :] += r3[k, i].astype(F32)

        each(na - 1, add)
        for r in range(k * per, (k + 1) * per):
            out[:, r * blk : (r + 1) * blk] = final[r * rows : (r + 1) * rows, :].astype(out.dtype)

    steps = (step1, step2, step3, step4)
    for tick in range(chunks + 3):
        for late, step in enumerate(steps):
            if 0 <= tick - late < chunks:
                step(tick - late)

    each(na - 1, lambda i: copy_a(i).wait_send())
    each(na, lambda i: copy_b(i).wait_send())
    each(na, lambda i: copy_c(i, 0).wait_send())
    each(na, lambda i: copy_c(i, 1).wait_send())
    for k in range(chunks):
        send1(k).wait_send()
        send2(k).wait_send()
        each(na - 1, lambda i: send3(k, i).wait_send())


def solution(mesh):
    n = mesh.shape["hid"]
    chunks = 4

    def shards(tokens, norm_gain, curve_point, gate_t, up_t, down_t, gate_i, up_i, down_i, counts):
        rows, width = tokens.shape
        cap, blk = gate_t.shape[2], gate_t.shape[-1]
        nb = width // blk
        msg = nb * rows
        part = msg // chunks
        na, half = n // 4, n // 2
        smem = pl.BlockSpec(memory_space=pltpu.SMEM)
        vmem = pl.BlockSpec(memory_space=pltpu.VMEM)
        hbm = pl.BlockSpec(memory_space=pl.ANY)
        dma = pltpu.SemaphoreType.DMA
        return pl.pallas_call(
            functools.partial(kernel, n, chunks),
            out_shape=jax.ShapeDtypeStruct((rows, width), BF16),
            in_specs=[vmem, vmem, smem, smem, smem, smem, smem, hbm, hbm, hbm],
            out_specs=vmem,
            scratch_shapes=[
                pltpu.VMEM((3, cap, blk, blk), BF16),
                pltpu.VMEM((3, cap, blk, blk), BF16),
                pltpu.VMEM((3 * cap + 1, blk, blk), BF16),
                pltpu.VMEM((n, msg, blk), BF16),
                pltpu.VMEM((n * msg, blk), F32),
                pltpu.VMEM((nb + 1, rows * n, blk), BF16),
                pltpu.VMEM((msg, blk), F32),
                pltpu.VMEM((chunks, half, part, blk), BF16),
                pltpu.VMEM((chunks, half, part, blk), BF16),
                pltpu.VMEM((chunks, na, part, blk), BF16),
                pltpu.VMEM((chunks, na, part, blk), BF16),
                pltpu.VMEM((chunks, na - 1, part, blk), BF16),
                pltpu.VMEM((chunks, na - 1, part, blk), BF16),
                pltpu.VMEM((8, 128), jnp.int32),
                pltpu.SMEM((8, 128), jnp.int32),
                dma((3, 3)),
                dma(()),
                dma((na - 1,)),
                dma((na - 1,)),
                dma((na,)),
                dma((na,)),
                dma((2 * na,)),
                dma((2 * na,)),
                dma((chunks,)),
                dma((chunks,)),
                dma((chunks,)),
                dma((chunks,)),
                dma((chunks, na - 1)),
                dma((chunks, na - 1)),
            ],
            compiler_params=pltpu.CompilerParams(
                collective_id=0, has_side_effects=True, vmem_limit_bytes=56 * 2**20
            ),
        )(
            tokens,
            norm_gain.reshape(1, width),
            curve_point,
            gate_i,
            up_i,
            down_i,
            counts,
            gate_t,
            up_t,
            down_t,
        )

    return jax.shard_map(
        shards,
        mesh=mesh,
        in_specs=(
            P(("group", "hid"), None),
            P(),
            P(),
            P(None, "hid", None, None, None),
            P(None, "hid", None, None, None),
            P(None, "hid", None, None, None),
            P(None, "hid", None),
            P(None, "hid", None),
            P(None, "hid", None),
            P(None, None, "hid"),
        ),
        out_specs=P(("group", "hid"), None),
        check_vma=False,
    )
```

time: 135 us -> 38.1 us (0.28)
  blocking collectives: 94.1 us -> 0 us
  Pallas kernels: 0 us -> 33 us
  other arithmetic: 16.7 us -> 0 us
  matrix products: 14.4 us -> 0 us
  local copies, waits for them, and re-layouts: 7.3 us -> 4.11 us
    unnamed x1 -> x0, blocking collectives: 69.5 us -> none
    pallas_call x0 -> x1, Pallas kernels: none -> 33 us  [shards(): pl.pallas_call(functools.partial(kernel, n, chunks), out_shape=jax.ShapeD...]
    all_gather x1 -> x0, blocking collectives: 24.6 us -> none  [shards(): piece_rows = lax.all_gather(normed, 'hid', axis=0, tiled=True)]
    dot_general x9 -> x0, matrix products: 14.4 us -> none  [the longest x6 9.74 us: packed_in(): jnp.einsum('rsk,skh->rh', chosen, tile_set, preferred_element_type=jnp.fl...]
    scatter-add x3 -> x0, other arithmetic: 7.71 us -> none  [packed_out(): return running.at[:, block_ids].add(product)]
    lt x9 -> x0, other arithmetic: 5.67 us -> none  [shards(): slot_ids < kept_counts[matrix_id, control, 0]]
    gather x6 -> x0, local copies, waits for them, and re-layouts: 3.62 us -> none  [packed_in(): chosen = jnp.take(blocks, block_ids, axis=1)]
    unnamed x7 -> x2, local copies, waits for them, and re-layouts: 0.6 us -> 2.76 us
where the time goes in v1:
time: 38.1 us; the launch traced here: 37.8 us
  Pallas kernels  33 us (87%)
  local copies, waits for them, and re-layouts  4.11 us (11%)
  between operations  0.66 us (2%)
    pallas_call x1, Pallas kernels, shards(): pl.pallas_call(functools.partial(kernel, n, chunks), out_shape=jax.ShapeD...  33 us
    unnamed x2, local copies, waits for them, and re-layouts  2.76 us
    reshape x1, local copies, waits for them, and re-layouts, shards(): norm_gain.reshape(1, width)  1.35 us

profile of v1, /device:TPU:0, one launch (start us, length us, event | category | flops | bytes accessed | tf_op | source)
XLA Modules:
  0.0 37.8 jit_solution(6912801890208611704)
XLA Ops:
  0.7 1.4 %copy.11.counts = s32[3,3,1]{2,1,0:T(4,128)} copy(s32[3,3,1]{1,2,0:T(1,128)} %param.19) | data formatting | bytes 72 | tf_op args[9]
  2.0 1.3 %reshape.3.gain = bf16[1,8192]{1,0:T(2,128)(2,1)} reshape(bf16[8192]{0:T(1024)(128)(2,1)} %param.11) | data formatting | bytes 32768 | tf_op jit(solution)/shard_map/reshape | solution.py:377
  3.4 33.0 %shard_map.100 = bf16[2,8192]{1,0:T(2,128)(2,1)} custom-call(bf16[2,8192]{1,0:T(2,128)(2,1)} %tok.1, bf16[1,8192]{1,0:T(2,128)(2,1)} %reshape.3.gain, f32[1]{0:T(128)S(6)} %copy.13.point_ref, s32[3,1,36]{2,1,0:T(1,128)} %gate_idx.1, s32[3,1,36]{2,1,0:T(1,128)} %up_idx.1, s32[3,1,36]{2,1,0:T(1,128)} %down_idx.1, s32[3,3,1]{2,1,0:T(4,128)} %copy.11.counts, ...), custom_call_target="tpu_custom_call" | custom-call | tf_op jit(solution)/shard_map/pallas_call | solution.py:336
  36.4 1.4 %copy.14 = bf16[2,8192]{1,0:T(2,128)(2,1)} copy(bf16[2,8192]{1,0:T(2,128)(2,1)} %shard_map.100) | data formatting | bytes 65536

commit v2 on v1

--- a/solution.py
+++ b/solution.py
@@ -32,10 +32,10 @@
     tok,
     gain,
     point_ref,
-    gate_idx,
-    up_idx,
-    down_idx,
-    counts,
+    gate_idx_hbm,
+    up_idx_hbm,
+    down_idx_hbm,
+    counts_hbm,
     gate_hbm,
     up_hbm,
     down_hbm,
@@ -53,8 +53,14 @@
     r2,
     s3,
     r3,
+    gain_rows,
+    gate_idx,
+    up_idx,
+    down_idx,
+    counts,
     inv_v,
     inv_s,
+    list_sem,
     w_sem,
     inv_sem,
     ga_s,
@@ -90,6 +96,13 @@
     def peer(a_, b_, core_):
         return {"hid": a_ * 4 + b_ * 2 + core_}
 
+    def near(i):
+        total, bit = 0, 1
+        while bit < na:
+            total = total + lax.rem(a // bit + i // bit, 2) * bit
+            bit *= 2
+        return total
+
     core_peer = peer(a, b, 1 - core)
     b_peer = peer(a, 1 - b, core)
     me = place(core, b, a)
@@ -99,6 +112,14 @@
             src_ref=src, dst_ref=dst, send_sem=send, recv_sem=recv, device_id=to, device_id_type=MESH
         )
 
+    lists = [
+        pltpu.make_async_copy(src, dst, list_sem.at[i])
+        for i, (src, dst) in enumerate(
+            ((down_idx_hbm, down_idx), (counts_hbm, counts), (gate_idx_hbm, gate_idx), (up_idx_hbm, up_idx))
+        )
+    ]
+    for copy in lists:
+        copy.start()
     loads = []
     for m, (src, dst) in enumerate(((gate_hbm, gate_w), (up_hbm, up_w))):
         for c in range(3):
@@ -113,7 +134,7 @@
     barrier = pltpu.get_barrier_semaphore()
 
     def greet(i):
-        to = peer(lax.rem(a + 1 + i, na), b, core)
+        to = peer(near(i + 1), b, core)
         pl.semaphore_signal(barrier, inc=1, device_id=to, device_id_type=MESH)
 
     each(na - 1, greet)
@@ -122,37 +143,39 @@
 
     x = tok[...].astype(F32)
     mean_square = jnp.sum(x * x, axis=-1, keepdims=True) / width
-    x = x * lax.rsqrt(mean_square + EPS) * gain[...].astype(F32)
+    x = x * lax.rsqrt(mean_square + EPS)
     for r in range(nb):
         final[r * rows : (r + 1) * rows, :] = x[:, r * blk : (r + 1) * blk]
-    gathered[me] = final[...].astype(BF16)
+    for t in range(rows):
+        gain_rows[pl.ds(t, nb, stride=rows), :] = gain[...].astype(F32)
+    gathered[me] = (final[...] * gain_rows[...]).astype(BF16)
 
     pl.semaphore_wait(barrier, na + 1)
 
     def copy_a(i):
         blk_ref = gathered.at[me]
-        return remote(blk_ref, blk_ref, ga_s.at[i], ga_r.at[i], peer(lax.rem(a + 1 + i, na), b, core))
+        return remote(blk_ref, blk_ref, ga_s.at[i], ga_r.at[i], peer(near(i + 1), b, core))
 
     def copy_b(i):
-        blk_ref = gathered.at[place(core, b, lax.rem(a - i + na, na))]
+        blk_ref = gathered.at[place(core, b, near(i))]
         return remote(blk_ref, blk_ref, gb_s.at[i], gb_r.at[i], b_peer)
 
     def copy_c(i, b_):
-        at = place(core, b if b_ == 0 else 1 - b, lax.rem(a - i + na, na))
+        at = place(core, b if b_ == 0 else 1 - b, near(i))
         blk_ref = gathered.at[at]
         sem = i + b_ * na
         return remote(blk_ref, blk_ref, gc_s.at[sem], gc_r.at[sem], core_peer)
 
     def got_a(i):
-        ref = gathered.at[place(core, b, lax.rem(a - 1 - i + na, na))]
+        ref = gathered.at[place(core, b, near(i + 1))]
         remote(ref, ref, ga_s.at[i], ga_r.at[i], b_peer).wait_recv()
 
     def got_b(i):
-        ref = gathered.at[place(core, 1 - b, lax.rem(a - i + na, na))]
+        ref = gathered.at[place(core, 1 - b, near(i))]
         remote(ref, ref, gb_s.at[i], gb_r.at[i], b_peer).wait_recv()
 
     def got_c(i, b_):
-        ref = gathered.at[place(1 - core, b if b_ == 0 else 1 - b, lax.rem(a - i + na, na))]
+        ref = gathered.at[place(1 - core, b if b_ == 0 else 1 - b, near(i))]
         sem = i + b_ * na
         remote(ref, ref, gc_s.at[sem], gc_r.at[sem], core_peer).wait_recv()
 
@@ -161,11 +184,13 @@
     copy_c(0, 0).start()
 
     zero_tile = 3 * cap
+    for copy in lists[:2]:
+        copy.wait()
     lane = lax.broadcasted_iota(jnp.int32, (8, 128), 1)
     line = lax.broadcasted_iota(jnp.int32, (8, 128), 0)
     table = jnp.full((8, 128), zero_tile, jnp.int32)
     for c in range(3):
-        kept = counts[2, c, 0]
+        kept = counts[2, 0, c]
         row = jnp.full((8, 128), zero_tile, jnp.int32)
         for s in range(cap):
             target = jnp.where(s < kept, down_idx[c, 0, s], -1)
@@ -177,25 +202,32 @@
     blocks[nb] = jnp.zeros(blocks.shape[1:], BF16)
     down_w[zero_tile] = jnp.zeros((blk, blk), BF16)
 
+    def widen(p):
+        stage[pl.ds(pl.multiple_of(p * msg, msg), msg), :] = gathered[p].astype(F32)
+
+    widen(me)
+
     def on_a(i):
         got_a(i)
         copy_b(i + 1).start()
         copy_c(i + 1, 0).start()
+        widen(place(core, b, near(i + 1)))
 
     each(na - 1, on_a)
 
     def on_b(i):
         got_b(i)
         copy_c(i, 1).start()
+        widen(place(core, 1 - b, near(i)))
 
     each(na, on_b)
-    each(na, lambda i: got_c(i, 0))
-    each(na, lambda i: got_c(i, 1))
-
-    def widen(p):
-        stage[pl.ds(p * msg, msg), :] = gathered[p].astype(F32)
-
-    each(n, widen)
+
+    def on_c(i, b_):
+        got_c(i, b_)
+        widen(place(1 - core, b if b_ == 0 else 1 - b, near(i)))
+
+    each(na, lambda i: on_c(i, 0))
+    each(na, lambda i: on_c(i, 1))
 
     def regroup(g):
         for d in range(8):
@@ -208,12 +240,15 @@
     point = point_ref[0]
     coef = ((1.0 - point) * (1.0 - point), 2.0 * point * (1.0 - point), point * point)
 
+    for copy in lists[2:]:
+        copy.wait()
+
     def project(m, idx, w):
         total = jnp.zeros((rows * n, blk), F32)
         group = 12
         for c in range(3):
             loads[m * 3 + c].wait()
-            kept = counts[m, c, 0]
+            kept = counts[m, 0, c]
             acc = jnp.zeros((rows * n, blk), F32)
             for g in range(0, cap, group):
                 size = min(group, cap - g)
@@ -257,7 +292,7 @@
         return remote(s2.at[k], r2.at[k], s2_s.at[k], s2_r.at[k], b_peer)
 
     def send3(k, i):
-        to = peer(lax.rem(a + 1 + i, na), b, core)
+        to = peer(near(i + 1), b, core)
         return remote(s3.at[k, i], r3.at[k, i], s3_s.at[k, i], s3_r.at[k, i], to)
 
     def step1(k):
@@ -287,7 +322,7 @@
             return piece(core * half + at, k) + r1[k, at].astype(F32) + r2[k, q].astype(F32)
 
         def pack(i):
-            s3[k, i] = value(lax.rem(a + 1 + i, na)).astype(BF16)
+            s3[k, i] = value(near(i + 1)).astype(BF16)
             send3(k, i).start()
 
         each(na - 1, pack)
@@ -302,11 +337,9 @@
         for r in range(k * per, (k + 1) * per):
             out[:, r * blk : (r + 1) * blk] = final[r * rows : (r + 1) * rows, :].astype(out.dtype)
 
-    steps = (step1, step2, step3, step4)
-    for tick in range(chunks + 3):
-        for late, step in enumerate(steps):
-            if 0 <= tick - late < chunks:
-                step(tick - late)
+    for step in (step1, step2, step3, step4):
+        for k in range(chunks):
+            step(k)
 
     each(na - 1, lambda i: copy_a(i).wait_send())
     each(na, lambda i: copy_b(i).wait_send())
@@ -336,7 +369,7 @@
         return pl.pallas_call(
             functools.partial(kernel, n, chunks),
             out_shape=jax.ShapeDtypeStruct((rows, width), BF16),
-            in_specs=[vmem, vmem, smem, smem, smem, smem, smem, hbm, hbm, hbm],
+            in_specs=[vmem, vmem, smem] + [hbm] * 7,
             out_specs=vmem,
             scratch_shapes=[
                 pltpu.VMEM((3, cap, blk, blk), BF16),
@@ -352,8 +385,14 @@
                 pltpu.VMEM((chunks, na, part, blk), BF16),
                 pltpu.VMEM((chunks, na - 1, part, blk), BF16),
                 pltpu.VMEM((chunks, na - 1, part, blk), BF16),
+                pltpu.VMEM((msg, blk), F32),
+                pltpu.SMEM(gate_i.shape, jnp.int32),
+                pltpu.SMEM(up_i.shape, jnp.int32),
+                pltpu.SMEM(down_i.shape, jnp.int32),
+                pltpu.SMEM((3, 1, 3), jnp.int32),
                 pltpu.VMEM((8, 128), jnp.int32),
                 pltpu.SMEM((8, 128), jnp.int32),
+                dma((4,)),
                 dma((3, 3)),
                 dma(()),
                 dma((na - 1,)),
@@ -374,12 +413,12 @@
             ),
         )(
             tokens,
-            norm_gain.reshape(1, width),
+            norm_gain.reshape(nb, blk),
             curve_point,
             gate_i,
             up_i,
             down_i,
-            counts,
+            jnp.transpose(counts, (0, 2, 1)),
             gate_t,
             up_t,
             down_t,

time: 38.1 us -> 31.1 us (0.82)
  Pallas kernels: 33 us -> 28.7 us
  local copies, waits for them, and re-layouts: 4.11 us -> 1.4 us
    pallas_call x1, Pallas kernels: 33 us -> 28.7 us  [shards(): pl.pallas_call(functools.partial(kernel, n, chunks), out_shape=jax.ShapeD...]
    unnamed x2 -> x1, local copies, waits for them, and re-layouts: 2.76 us -> 1.4 us
    reshape x1 -> x0, local copies, waits for them, and re-layouts: 1.35 us -> none  [shards(): norm_gain.reshape(1, width)]
where the time goes in v2:
time: 31.1 us; the launch traced here: 30.8 us
  Pallas kernels  28.7 us (92%)
  local copies, waits for them, and re-layouts  1.4 us (5%)
  between operations  0.66 us (2%)
    pallas_call x1, Pallas kernels, shards(): pl.pallas_call(functools.partial(kernel, n, chunks), out_shape=jax.ShapeD...  28.7 us
    unnamed x1, local copies, waits for them, and re-layouts  1.4 us

profile of v2, /device:TPU:0, one launch (start us, length us, event | category | flops | bytes accessed | tf_op | source)
XLA Modules:
  0.0 30.8 jit_solution(2977635979390199318)
XLA Ops:
  0.7 28.7 %shard_map.100 = bf16[2,8192]{1,0:T(2,128)(2,1)} custom-call(bf16[2,8192]{1,0:T(2,128)(2,1)} %tok.1, bf16[64,128]{1,0:T(8,128)(2,1)} %bitcast.2, f32[1]{0:T(128)S(6)} %copy.12.point_ref, s32[3,1,36]{2,1,0:T(1,128)} %gate_idx_hbm.1, s32[3,1,36]{2,1,0:T(1,128)} %up_idx_hbm.1, s32[3,1,36]{2,1,0:T(1,128)} %down_idx_hbm.1, s32[3,1,3]{2,1,0:T(1,128)} %bitcast.3, ...), custom_call_target="tpu_custom_call" | custom-call | tf_op jit(solution)/shard_map/pallas_call | solution.py:369
  29.4 1.4 %copy.13 = bf16[2,8192]{1,0:T(2,128)(2,1)} copy(bf16[2,8192]{1,0:T(2,128)(2,1)} %shard_map.100) | data formatting | bytes 65536

commit v3 on v2

--- a/solution.py
+++ b/solution.py
@@ -29,8 +29,8 @@
 def kernel(
     n,
     chunks,
-    tok,
-    gain,
+    tok_hbm,
+    gain_hbm,
     point_ref,
     gate_idx_hbm,
     up_idx_hbm,
@@ -53,6 +53,8 @@
     r2,
     s3,
     r3,
+    tok,
+    gain,
     gain_rows,
     gate_idx,
     up_idx,
@@ -61,6 +63,7 @@
     inv_v,
     inv_s,
     list_sem,
+    tok_sem,
     w_sem,
     inv_sem,
     ga_s,
@@ -112,6 +115,23 @@
             src_ref=src, dst_ref=dst, send_sem=send, recv_sem=recv, device_id=to, device_id_type=MESH
         )
 
+    early = [
+        pltpu.make_async_copy(tok_hbm, tok, tok_sem.at[0]),
+        pltpu.make_async_copy(gain_hbm, gain, tok_sem.at[1]),
+    ]
+    for copy in early:
+        copy.start()
+
+    barrier = pltpu.get_barrier_semaphore()
+
+    def greet(i):
+        to = peer(near(i + 1), b, core)
+        pl.semaphore_signal(barrier, inc=1, device_id=to, device_id_type=MESH)
+
+    each(na - 1, greet)
+    pl.semaphore_signal(barrier, inc=1, device_id=b_peer, device_id_type=MESH)
+    pl.semaphore_signal(barrier, inc=1, device_id=core_peer, device_id_type=MESH)
+
     lists = [
         pltpu.make_async_copy(src, dst, list_sem.at[i])
         for i, (src, dst) in enumerate(
@@ -131,15 +151,8 @@
     for copy in loads:
         copy.start()
 
-    barrier = pltpu.get_barrier_semaphore()
-
-    def greet(i):
-        to = peer(near(i + 1), b, core)
-        pl.semaphore_signal(barrier, inc=1, device_id=to, device_id_type=MESH)
-
-    each(na - 1, greet)
-    pl.semaphore_signal(barrier, inc=1, device_id=b_peer, device_id_type=MESH)
-    pl.semaphore_signal(barrier, inc=1, device_id=core_peer, device_id_type=MESH)
+    for copy in early:
+        copy.wait()
 
     x = tok[...].astype(F32)
     mean_square = jnp.sum(x * x, axis=-1, keepdims=True) / width
@@ -369,7 +382,7 @@
         return pl.pallas_call(
             functools.partial(kernel, n, chunks),
             out_shape=jax.ShapeDtypeStruct((rows, width), BF16),
-            in_specs=[vmem, vmem, smem] + [hbm] * 7,
+            in_specs=[hbm, hbm, smem] + [hbm] * 7,
             out_specs=vmem,
             scratch_shapes=[
                 pltpu.VMEM((3, cap, blk, blk), BF16),
@@ -385,6 +398,8 @@
                 pltpu.VMEM((chunks, na, part, blk), BF16),
                 pltpu.VMEM((chunks, na - 1, part, blk), BF16),
                 pltpu.VMEM((chunks, na - 1, part, blk), BF16),
+                pltpu.VMEM((rows, width), BF16),
+                pltpu.VMEM((nb, blk), BF16),
                 pltpu.VMEM((msg, blk), F32),
                 pltpu.SMEM(gate_i.shape, jnp.int32),
                 pltpu.SMEM(up_i.shape, jnp.int32),
@@ -393,6 +408,7 @@
                 pltpu.VMEM((8, 128), jnp.int32),
                 pltpu.SMEM((8, 128), jnp.int32),
                 dma((4,)),
+                dma((2,)),
                 dma((3, 3)),
                 dma(()),
                 dma((na - 1,)),

time: 31.1 us -> 30.3 us (0.974)
  Pallas kernels: 28.7 us -> 28.1 us
    pallas_call x1, Pallas kernels: 28.7 us -> 28.1 us  [shards(): pl.pallas_call(functools.partial(kernel, n, chunks), out_shape=jax.ShapeD...]
where the time goes in v3:
time: 30.3 us; the launch traced here: 30.1 us
  Pallas kernels  28.1 us (93%)
  local copies, waits for them, and re-layouts  1.4 us (5%)
  between operations  0.66 us (2%)
    pallas_call x1, Pallas kernels, shards(): pl.pallas_call(functools.partial(kernel, n, chunks), out_shape=jax.ShapeD...  28.1 us
    unnamed x1, local copies, waits for them, and re-layouts  1.4 us

profile of v3, /device:TPU:0, one launch (start us, length us, event | category | flops | bytes accessed | tf_op | source)
XLA Modules:
  0.0 30.1 jit_solution(4837684192748197224)
XLA Ops:
  0.7 28.1 %shard_map.100 = bf16[2,8192]{1,0:T(2,128)(2,1)} custom-call(bf16[2,8192]{1,0:T(2,128)(2,1)} %tok_hbm.1, bf16[64,128]{1,0:T(8,128)(2,1)} %bitcast.2, f32[1]{0:T(128)S(6)} %copy.12.point_ref, s32[3,1,36]{2,1,0:T(1,128)} %gate_idx_hbm.1, s32[3,1,36]{2,1,0:T(1,128)} %up_idx_hbm.1, s32[3,1,36]{2,1,0:T(1,128)} %down_idx_hbm.1, s32[3,1,3]{2,1,0:T(1,128)} %bitcast.3, ...), custom_call_target="tpu_custom_call" | custom-call | tf_op jit(solution)/shard_map/pallas_call | solution.py:382
  28.7 1.4 %copy.13 = bf16[2,8192]{1,0:T(2,128)(2,1)} copy(bf16[2,8192]{1,0:T(2,128)(2,1)} %shard_map.100) | data formatting | bytes 65536

commit v4 on v3

--- a/solution.py
+++ b/solution.py
@@ -350,7 +350,12 @@
         for r in range(k * per, (k + 1) * per):
             out[:, r * blk : (r + 1) * blk] = final[r * rows : (r + 1) * rows, :].astype(out.dtype)
 
-    for step in (step1, step2, step3, step4):
+    for k in range(chunks + 1):
+        if k < chunks:
+            step1(k)
+        if k >= 1:
+            step2(k - 1)
+    for step in (step3, step4):
         for k in range(chunks):
             step(k)
 

time: 30.3 us -> 30.2 us (level)
  no operation moved by 1% of the time
where the time goes in v4:
time: 30.2 us; the launch traced here: 30 us
  Pallas kernels  28 us (93%)
  local copies, waits for them, and re-layouts  1.4 us (5%)
  between operations  0.66 us (2%)
    pallas_call x1, Pallas kernels, shards(): pl.pallas_call(functools.partial(kernel, n, chunks), out_shape=jax.ShapeD...  28 us
    unnamed x1, local copies, waits for them, and re-layouts  1.4 us

profile of v4, /device:TPU:0, one launch (start us, length us, event | category | flops | bytes accessed | tf_op | source)
XLA Modules:
  0.0 30.0 jit_solution(3430212784747641417)
XLA Ops:
  0.7 28.0 %shard_map.100 = bf16[2,8192]{1,0:T(2,128)(2,1)} custom-call(bf16[2,8192]{1,0:T(2,128)(2,1)} %tok_hbm.1, bf16[64,128]{1,0:T(8,128)(2,1)} %bitcast.2, f32[1]{0:T(128)S(6)} %copy.12.point_ref, s32[3,1,36]{2,1,0:T(1,128)} %gate_idx_hbm.1, s32[3,1,36]{2,1,0:T(1,128)} %up_idx_hbm.1, s32[3,1,36]{2,1,0:T(1,128)} %down_idx_hbm.1, s32[3,1,3]{2,1,0:T(1,128)} %bitcast.3, ...), custom_call_target="tpu_custom_call" | custom-call | tf_op jit(solution)/shard_map/pallas_call | solution.py:387
  28.6 1.4 %copy.13 = bf16[2,8192]{1,0:T(2,128)(2,1)} copy(bf16[2,8192]{1,0:T(2,128)(2,1)} %shard_map.100) | data formatting | bytes 65536

commit v5 on v3

--- a/solution.py
+++ b/solution.py
@@ -285,13 +285,16 @@
 
     def down(k):
         def some(g):
+            first = k * per + g * 4
+            total = jnp.zeros((rows * n, 4 * blk), F32)
+            for c in range(3):
+                tiles = jnp.concatenate([down_w[inv_s[c, first + d]] for d in range(4)], axis=1)
+                total = total + coef[c] * jnp.dot(hidden, tiles, preferred_element_type=F32)
             for d in range(4):
-                r = k * per + g * 4 + d
-                total = jnp.zeros((rows * n, blk), F32)
-                for c in range(3):
-                    total = total + coef[c] * jnp.dot(hidden, down_w[inv_s[c, r]], preferred_element_type=F32)
                 for t in range(rows):
-                    stage[pl.ds(r * rows + t, n, stride=msg), :] = total[t * n : (t + 1) * n]
+                    stage[pl.ds((first + d) * rows + t, n, stride=msg), :] = total[
+                        t * n : (t + 1) * n, d * blk : (d + 1) * blk
+                    ]
 
         each(per // 4, some)
 

time: 30.3 us -> 30.1 us (level)
  no operation moved by 1% of the time
where the time goes in v5:
time: 30.1 us; the launch traced here: 30 us
  Pallas kernels  27.9 us (93%)
  local copies, waits for them, and re-layouts  1.4 us (5%)
  between operations  0.66 us (2%)
    pallas_call x1, Pallas kernels, shards(): pl.pallas_call(functools.partial(kernel, n, chunks), out_shape=jax.ShapeD...  27.9 us
    unnamed x1, local copies, waits for them, and re-layouts  1.4 us

profile of v5, /device:TPU:0, one launch (start us, length us, event | category | flops | bytes accessed | tf_op | source)
XLA Modules:
  0.0 30.0 jit_solution(15816504630408947919)
XLA Ops:
  0.7 27.9 %shard_map.100 = bf16[2,8192]{1,0:T(2,128)(2,1)} custom-call(bf16[2,8192]{1,0:T(2,128)(2,1)} %tok_hbm.1, bf16[64,128]{1,0:T(8,128)(2,1)} %bitcast.2, f32[1]{0:T(128)S(6)} %copy.12.point_ref, s32[3,1,36]{2,1,0:T(1,128)} %gate_idx_hbm.1, s32[3,1,36]{2,1,0:T(1,128)} %up_idx_hbm.1, s32[3,1,36]{2,1,0:T(1,128)} %down_idx_hbm.1, s32[3,1,3]{2,1,0:T(1,128)} %bitcast.3, ...), custom_call_target="tpu_custom_call" | custom-call | tf_op jit(solution)/shard_map/pallas_call | solution.py:385
  28.6 1.4 %copy.13 = bf16[2,8192]{1,0:T(2,128)(2,1)} copy(bf16[2,8192]{1,0:T(2,128)(2,1)} %shard_map.100) | data formatting | bytes 65536
